TPU v7x, 32 devices: a whole 2x2x4 slice. The times are simulated.
32 devices in a mesh: tm: 4 (over x, core), expert: 8 (over z, y).
Axes of the slice: x: 2, y: 2, z: 4, core: 2. Of those that a mesh axis runs over, the one named last changes fastest.
Arguments:
- tokens: bfloat16 [8, 32, 64, 1280], P('expert', 'tm'), may hold values from -6 to 6
- time_taps: float32 [3, 1280], replicated, may hold values from -3 to 3
- norm_gain: float32 [1280], replicated, may hold values from 0.5 to 1.5
- expert_ids: int32 [8, 2048, 2], P('expert'), may hold values from 0 to 7, as said below
- priority_ranks: int32 [8, 2048, 2], P('expert'), may hold values from 0 to 256, as said below
- keep_mask: int32 [8, 2048, 2], P('expert'), may hold values from 0 to 1, as said below
- gate_weights: float32 [8, 2048, 2], P('expert'), may hold values from 0.2 to 1
- up_weight: bfloat16 [8, 1280, 5120], P('expert', None, 'tm'), may hold values from -0.15625 to 0.15625
- down_weight: bfloat16 [8, 5120, 1280], P('expert', 'tm'), may hold values from -0.078125 to 0.078125
- attn_gain: float32 [1280], replicated, may hold values from 0.5 to 1.5
- qkv_weight: bfloat16 [3, 1280, 1280], P(None, None, 'tm'), may hold values from -0.15625 to 0.15625
Outputs:
- stream: bfloat16 [8, 32, 64, 1280], P('expert', 'tm')
- qkv_rows: bfloat16 [3, 8, 2048, 1280], P(None, 'expert', None, 'tm')
Inputs may be any that keep to these rules, and one draw needn't show every extreme that they name: `expert_ids`: the two experts of a token differ. priority_ranks[b, t, k] counts the assignments of clip b to the same expert that come earlier in batch-priority order, and is given as 256 where that count is 256 or more; every first choice of a clip comes before every second choice. Within a clip the kept assignments of one expert have distinct ranks. keep_mask is 1 exactly where priority_ranks < 256, so every expert receives at most 256 rows from each clip, and exactly 256 for some expert of every clip.
All inputs are finite; a program needn't handle non-finite values.
Results may differ from a plain program's by a relative error of at most 0.008.
Values may be sent and summed in bfloat16 or wider, within the bound.
No kernel may reach another device: no remote copies, remote signals or barrier semaphores. Data moves between devices by JAX's collectives and lax.ppermute only.
A program may use at most 128 MiB of HBM per device.

v0:
```python
import jax
import jax.numpy as jnp
from jax import lax
from jax.sharding import PartitionSpec as P

eps = 1e-06


def passed_along(value, axis, steps):
    count = lax.axis_size(axis)
    leading, last = (max(0, -steps), min(count, count - steps))
    return lax.ppermute(value, axis, [(source, source + steps) for source in range(leading, last)])


def layer_norm(values, gain):
    center = values - jnp.mean(values, -1, keepdims=True)
    spread = jnp.mean(center * center, -1, keepdims=True)
    return center * lax.rsqrt(spread + eps) * gain


def temporal_mix(extended, time_taps):
    widened = extended.astype(jnp.float32)
    return (
        time_taps[0] * widened[:, 2:]
        + time_taps[1] * widened[:, 1:-1]
        + time_taps[2] * widened[:, :-2]
    ).astype(jnp.bfloat16)


def local(
    tokens,
    time_taps,
    norm_gain,
    expert_ids,
    priority_ranks,
    keep_mask,
    gate_weights,
    up_weight,
    down_weight,
    attn_gain,
    qkv_weight,
):
    frames_here = tokens.shape[1]
    width = tokens.shape[3]
    earlier = passed_along(tokens[:, frames_here - 2 :], "tm", 1)
    local_mix = temporal_mix(jnp.concatenate([earlier, tokens], 1), time_taps)
    mixed = lax.all_gather(local_mix, "tm", axis=1, tiled=True)
    clip_rows = mixed.reshape(-1, width)
    row_count = clip_rows.shape[0]
    choices_per = expert_ids.shape[2]
    experts = lax.axis_size("expert")
    capacity = row_count * choices_per // (2 * experts)
    normed = layer_norm(clip_rows.astype(jnp.float32), norm_gain).astype(jnp.bfloat16)
    slot_index = jnp.where(
        keep_mask[0] == 1, expert_ids[0] * capacity + priority_ranks[0], experts * capacity
    )
    token_index = jnp.broadcast_to(
        jnp.arange(row_count, dtype=jnp.int32)[:, None], (row_count, choices_per)
    )
    source = (
        jnp.full((experts * capacity + 1,), row_count, jnp.int32)
        .at[slot_index.reshape(-1)]
        .set(token_index.reshape(-1))[: experts * capacity]
    )
    with_zero = jnp.concatenate([normed, jnp.zeros((1, width), jnp.bfloat16)], 0)
    outgoing = with_zero[source].reshape(experts, capacity, width)
    arrived = lax.all_to_all(outgoing, "expert", split_axis=0, concat_axis=0, tiled=True)
    hidden = jax.nn.gelu(
        jnp.dot(arrived.reshape(-1, width), up_weight[0], preferred_element_type=jnp.float32)
    ).astype(jnp.bfloat16)
    partial_value = jnp.dot(hidden, down_weight[0], preferred_element_type=jnp.float32).reshape(
        experts, capacity, width
    )
    slot_share = lax.psum_scatter(
        partial_value.astype(jnp.bfloat16), "tm", scatter_dimension=1, tiled=True
    )
    returned = lax.all_to_all(slot_share, "expert", split_axis=0, concat_axis=0, tiled=True)
    expert_out = lax.all_gather(returned, "tm", axis=1, tiled=True)
    table = jnp.concatenate([expert_out.reshape(-1, width), jnp.zeros((1, width), jnp.bfloat16)], 0)
    picked = table[slot_index]
    weight = jnp.where(keep_mask[0] == 1, gate_weights[0], 0.0)
    stream_full = (
        clip_rows.astype(jnp.float32) + jnp.sum(weight[:, :, None] * picked.astype(jnp.float32), 1)
    ).astype(jnp.bfloat16)
    attn_in = layer_norm(stream_full.astype(jnp.float32), attn_gain).astype(jnp.bfloat16)
    qkv_rows = jnp.stack(
        [
            jnp.dot(attn_in, qkv_weight[component], preferred_element_type=jnp.float32)
            for component in range(3)
        ]
    ).astype(jnp.bfloat16)[:, None]
    stream_view = stream_full.reshape(mixed.shape)
    own_frames = lax.dynamic_slice_in_dim(
        stream_view, lax.axis_index("tm") * frames_here, frames_here, 1
    )
    return (own_frames, qkv_rows)


def solution(mesh):
    in_specs = (
        P("expert", "tm", None, None),
        P(),
        P(),
        P("expert", None, None),
        P("expert", None, None),
        P("expert", None, None),
        P("expert", None, None),
        P("expert", None, "tm"),
        P("expert", "tm", None),
        P(),
        P(None, None, "tm"),
    )
    out_specs = (P("expert", "tm", None, None), P(None, "expert", None, "tm"))
    return jax.shard_map(local, mesh=mesh, in_specs=in_specs, out_specs=out_specs, check_vma=False)
```

profile of v0, /device:TPU:0, one launch (start us, length us, event | category | flops | bytes accessed | tf_op | source)
XLA Modules:
  0.0 552.3 jit_solution(6560600428523409846)
XLA Ops:
  8.4 2.4 collective-permute-start
  21.2 15.5 %scatter_custom_fusion = s32[2049]{0:T(1024)S(1)} fusion(s32[4096]{0:T(1024)S(1)} %bitcast.63, s32[4096]{0:T(1024)S(1)} %reshape.371, s32[]{:T(128)} %constant.21.clone.1), kind=kCustom, calls=%fused_computation.64 | custom fusion | bytes 8200 | tf_op jit(solution)/shard_map/scatter | solution.py:63
  36.7 26.5 %all-gather.3.cloned.1.call-done = bf16[1,32,64,1280]{3,2,0,1:T(8,128)(2,1)} async-done(((bf16[1,8,64,1280]{3,2,0,1:T(8,128)(2,1)}), bf16[1,32,64,1280]{3,2,0,1:T(8,128)(2,1)}) %all-gather.3.cloned.1.call-update) | async-done | bytes 5242896 | tf_op jit(solution)/shard_map/all_gather | solution.py:47
  63.2 3.2 convert_reduce_fusion.1
  66.5 4.0 multiply_reduce_fusion.1
  70.6 3.5 fusion.15
  74.1 2.7 concatenate.26
  76.7 15.2 %gather_fusion = bf16[2048,1280]{1,0:T(8,128)(2,1)} fusion(bf16[2049,1280]{1,0:T(8,128)(2,1)} %concatenate.26, s32[2048]{0:T(1024)S(1)} %fusion.33), kind=kCustom, calls=%fused_computation | custom fusion | bytes 10493952 | tf_op jit(solution)/shard_map/gather | solution.py:66
  92.0 121.5 %all_to_all.10 = bf16[8,256,1280]{2,1,0:T(8,128)(2,1)S(1)} all-to-all(bf16[8,256,1280]{2,1,0:T(8,128)(2,1)} %bitcast.55), channel_id=1, replica_groups=mesh['tm'=4,'expert'=8] {'expert'}, dimensions={0} | all-to-all | bytes 10485760 | tf_op jit(solution)/shard_map/all_to_all | solution.py:67
  213.5 8.4 %fusion.12 = bf16[2048,1280]{1,0:T(8,128)(2,1)S(1)} fusion(bf16[2048,1280]{1,0:T(8,128)(2,1)S(1)} %bitcast.57, bf16[1,1280,1280]{2,1,0:T(8,128)(2,1)S(1)} %copy-done), kind=kOutput, calls=%fused_computation.19 | convolution fusion | flops 6734479360 | bytes 13762560 | tf_op jit(solution)/shard_map/dot_general | solution.py:69
  221.9 8.7 %convolution_convert_fusion = bf16[8,256,1280]{2,1,0:T(8,128)(2,1)} fusion(bf16[8,256,1280]{2,1,0:T(8,128)(2,1)S(1)} %bitcast.64, bf16[1,1280,1280]{2,1,0:T(8,128)(2,1)S(1)} %copy-done.9), kind=kOutput, calls=%fused_computation.27 | convolution fusion | flops 6713507840 | bytes 13762560 | tf_op jit(solution)/shard_map/dot_general | solution.py:71
  230.7 49.6 %reduce-scatter.2.cloned.1.call-done = bf16[8,64,1280]{2,1,0:T(8,128)(2,1)} async-done(((bf16[8,256,1280]{2,1,0:T(8,128)(2,1)}), bf16[8,64,1280]{2,1,0:T(8,128)(2,1)}) %reduce-scatter.2.cloned.1.call-update) | async-done | bytes 1310736 | tf_op jit(solution)/shard_map/reduce_scatter | solution.py:74
  280.3 37.0 %all_to_all.11 = bf16[8,64,1280]{2,1,0:T(8,128)(2,1)} all-to-all(bf16[8,64,1280]{2,1,0:T(8,128)(2,1)} %reduce-scatter.2.cloned.1.call-done), channel_id=1, replica_groups=mesh['tm'=4,'expert'=8] {'expert'}, dimensions={0} | all-to-all | bytes 2621440 | tf_op jit(solution)/shard_map/all_to_all | solution.py:77
  318.6 37.4 %all-gather.5.cloned.1.call-done = bf16[8,256,1280]{2,1,0:T(8,128)(2,1)} async-done(((bf16[8,64,1280]{2,1,0:T(8,128)(2,1)}), bf16[8,256,1280]{2,1,0:T(8,128)(2,1)}) %all-gather.5.cloned.1.call-update) | async-done | bytes 5242896 | tf_op jit(solution)/shard_map/all_gather | solution.py:78
  356.0 5.1 concatenate.27
  361.1 26.1 %gather_fusion.1 = bf16[4096,1280]{1,0:T(8,128)(2,1)} fusion(bf16[2049,1280]{1,0:T(8,128)(2,1)} %concatenate.27, s32[4096]{0:T(1024)S(1)} %broadcast_clamp_fusion), kind=kCustom, calls=%fused_computation.1 | custom fusion | bytes 20987904 | tf_op jit(solution)/shard_map/gather | solution.py:80
  387.3 22.9 %reshape.377 = f32[2048,2,1280]{2,1,0:T(2,128)} reshape(bf16[4096,1280]{1,0:T(8,128)(2,1)} %gather_fusion.1) | data formatting | bytes 31457280 | tf_op jit(solution)/shard_map/convert_element_type | solution.py:83
  410.2 111.3 %multiply_reduce_fusion = f32[2048,1280]{1,0:T(8,128)} fusion(f32[2048,2,1280]{2,1,0:T(2,128)} %reshape.377, f32[2048,2]{1,0:T(8,128)S(1)} %copy.19), kind=kLoop, calls=%fused_computation.3 | loop fusion | flops 7864320 | bytes 31473664 | tf_op jit(solution)/shard_map/reduce_sum | solution.py:83
  521.4 8.9 %convert_reduce_fusion = (f32[32,64]{1,0:T(8,128)S(1)}, bf16[1,32,64,1280]{3,2,0,1:T(8,128)(2,1)}) fusion(f32[1,32,64,1280]{3,2,0,1:T(8,128)} %bitcast.54, bf16[1,32,64,1280]{3,2,0,1:T(8,128)(2,1)} %all-gather.3.cloned.1.call-done), kind=kLoop, calls=%fused_computation.6 | loop fusion | flops 13105152 | bytes 20979712 | tf_op jit(solution)/shard_map/reduce_sum | solution.py:16
  530.4 4.2 fusion.2
  534.6 2.2 fusion.4
  536.8 1.9 fusion.24
  540.6 1.9 fusion.26
  543.6 2.1 pad_maximum_fusion
  (53 shorter events, 16.1 us)
Async XLA Ops:
  7.2 206.4 %copy-start = (bf16[1,1280,1280]{2,1,0:T(8,128)(2,1)S(1)}, bf16[1,1280,1280]{2,1,0:T(8,128)(2,1)}, u32[]{:S(2)}) copy-start(bf16[1,1280,1280]{2,1,0:T(8,128)(2,1)} %param.18) | copy-start | bytes 9830404
  7.2 56.0 %all-gather.3.cloned.1.call-start = ((), (), s32[]{:S(2)}) async-start(), calls=%async_computation.3 | async-start | bytes 6553600 | tf_op jit(solution)/shard_map/all_gather | solution.py:47
  8.4 3.6 collective-permute-start
  13.5 1.7 copy-start.3
  13.5 1.7 copy-start.4
  13.5 1.7 copy-start.5
  15.1 265.2 %reduce-scatter.2.cloned.1.call-start = ((), (), s32[]{:S(2)}) async-start(), calls=%async_computation.4 | async-start | bytes 6553600 | tf_op jit(solution)/shard_map/reduce_scatter | solution.py:74
  36.7 33.9 %copy-start.7 = (f32[1280]{0:T(1024)S(1)}, f32[1280]{0:T(1024)}, u32[]{:S(2)}) copy-start(f32[1280]{0:T(1024)} %param.13) | copy-start | bytes 15364
  213.5 8.4 %copy-start.9 = (bf16[1,1280,1280]{2,1,0:T(8,128)(2,1)S(1)}, bf16[1,1280,1280]{2,1,0:T(8,128)(2,1)}, u32[]{:S(2)}) copy-start(bf16[1,1280,1280]{2,1,0:T(8,128)(2,1)} %param.19) | copy-start | bytes 9830404
  230.6 87.6 %copy-start.6 = (f32[1,2048,2]{1,2,0:T(2,128)S(1)}, f32[1,2048,2]{1,2,0:T(2,128)}, u32[]{:S(2)}) copy-start(f32[1,2048,2]{1,2,0:T(2,128)} %param.17) | copy-start | bytes 49156
  230.6 125.4 %all-gather.5.cloned.1.call-start = ((), (), s32[]{:S(2)}) async-start(), calls=%async_computation.5 | async-start | bytes 6553600 | tf_op jit(solution)/shard_map/all_gather | solution.py:78
  530.4 4.2 copy-start.2
  530.4 4.2 copy-start.8
  534.6 2.2 copy-start.10
  540.6 5.2 copy-start.1
Sparse Core Ops, SparseCore 0:
  15.2 47.9 all-gather.2
  230.8 49.4 reduce-scatter.1
  317.5 38.4 all-gather.4
where the time goes:
time: 553 us; the launch traced here: 552 us
  blocking collectives  159 us (29%)
  other arithmetic  143 us (26%)
  waiting for transfers between devices  114 us (21%)
  local copies, waits for them, and re-layouts  98.1 us (18%)
  matrix products  22.7 us (4%)
  between operations  14 us (3%)
    all_to_all x1, blocking collectives, local(): lax.all_to_all(outgoing, 'expert', split_axis=0, concat_axis=0, tiled=True)  122 us
    reduce_sum x1, other arithmetic, local(): jnp.sum(weight[:, :, None] * picked.astype(jnp.float32), 1)  111 us
    reduce_scatter x1, waiting for transfers between devices, local(): lax.psum_scatter(partial_value.astype(jnp.bfloat16), 'tm', scatter_dimens...  49.6 us
    all_gather x1, waiting for transfers between devices, local(): expert_out = lax.all_gather(returned, 'tm', axis=1, tiled=True)  37.4 us
    all_to_all x1, blocking collectives, local(): lax.all_to_all(slot_share, 'expert', split_axis=0, concat_axis=0, tiled=T...  37 us
    all_gather x1, waiting for transfers between devices, local(): mixed = lax.all_gather(local_mix, 'tm', axis=1, tiled=True)  26.5 us
    gather x1, local copies, waits for them, and re-layouts, local(): picked = table[slot_index]  26.1 us
    convert_element_type x1, local copies, waits for them, and re-layouts, local(): picked.astype(jnp.float32)  22.9 us
  transfers between devices with their start and end apart: 4, of which 4 were waited for; matrix products, arithmetic and copies ran while one was open for 4% of the time, Pallas kernels for 0%

commit v1 on v0

v1 whole, which is shorter than its diff:
```python
import functools

import jax
import jax.numpy as jnp
from jax import lax
from jax.experimental import pallas as pl
from jax.experimental.pallas import tpu as pltpu
from jax.sharding import PartitionSpec as P

eps = 1e-06
bf16 = jnp.bfloat16
f32 = jnp.float32
ROW_PARTS = 2
VMEM_BYTES = 56 * 1024 * 1024
HBM = pl.BlockSpec(memory_space=pl.ANY)
VMEM = pl.BlockSpec(memory_space=pltpu.VMEM)
SMEM = pl.BlockSpec(memory_space=pltpu.SMEM)


def column_parts(width):
    first = -(-(width // 2) // 128) * 128
    return [(0, first), (first, width - first)]


def call(kernel, out_shape, in_specs, out_specs, scratch, flops, moved, *args):
    return pl.pallas_call(
        kernel,
        out_shape=out_shape,
        in_specs=in_specs,
        out_specs=out_specs,
        scratch_shapes=scratch,
        compiler_params=pltpu.CompilerParams(vmem_limit_bytes=VMEM_BYTES),
        cost_estimate=pl.CostEstimate(flops=flops, bytes_accessed=moved, transcendentals=0),
    )(*args)


def swap(value, axis, distance):
    count = lax.axis_size(axis)
    return lax.ppermute(value, axis, [(i, i ^ distance) for i in range(count)])


def tile_of(rows):
    return 256 if rows % 256 == 0 else rows


def mix_kernel(blocks, patches, where_ref, taps_ref, *refs):
    tokens, mixed_ref, extended, sems = refs[:blocks], refs[-3], refs[-2], refs[-1]
    rows = tokens[0].shape[0]
    halo = 2 * patches
    copies = [
        pltpu.make_async_copy(
            tokens[i],
            extended.at[pl.ds(pl.multiple_of(halo + where_ref[i] * rows, patches), rows)],
            sems.at[i],
        )
        for i in range(blocks)
    ]
    for copy in copies:
        copy.start()
    extended[0:halo] = jnp.zeros((halo, extended.shape[1]), extended.dtype)
    for copy in copies:
        copy.wait()
    tile = patches

    def step(t, carry):
        start = pl.multiple_of(t * tile, tile)
        now = extended[pl.ds(start + halo, tile)].astype(f32)
        before = extended[pl.ds(start + patches, tile)].astype(f32)
        earlier = extended[pl.ds(start, tile)].astype(f32)
        mixed_ref[pl.ds(start, tile)] = (
            taps_ref[0:1] * now + taps_ref[1:2] * before + taps_ref[2:3] * earlier
        ).astype(bf16)
        return carry

    lax.fori_loop(0, blocks * rows // tile, step, 0)


def temporal_mix(tokens, places, taps, patches):
    blocks = len(tokens)
    rows, cols = tokens[0].shape
    total = blocks * rows
    return call(
        functools.partial(mix_kernel, blocks, patches),
        jax.ShapeDtypeStruct((total, cols), bf16),
        [SMEM, VMEM] + [HBM] * blocks,
        VMEM,
        [pltpu.VMEM((total + 2 * patches, cols), bf16), pltpu.SemaphoreType.DMA((blocks,))],
        total * cols * 5,
        total * cols * 4,
        places,
        taps,
        *tokens,
    )


def dispatch_kernel(per, where_ref, slot_ref, mixed_ref, *outs):
    rows = mixed_ref.shape[0]
    me, capacity, first = where_ref[0], where_ref[1], where_ref[2]
    code = slot_ref[...]
    owner = code // capacity
    rank = code - owner * capacity - first
    place = jnp.where((code >= 0) & (rank >= 0) & (rank < per), (owner ^ me) * per + rank, -1)
    together = max(1, 256 // per)
    for base in range(0, len(outs), together):
        group = outs[base : base + together]
        size = per * len(group)
        slots = lax.broadcasted_iota(jnp.int32, (size, rows), 0) + base * per
        hit = (slots == place[0:1]) | (slots == place[1:2])
        picked = jnp.dot(
            jnp.where(hit, 1.0, 0.0).astype(bf16), mixed_ref[...], preferred_element_type=f32
        ).astype(bf16)
        for i, out in enumerate(group):
            out[...] = picked[i * per : (i + 1) * per]


def dispatch(where, slots, mixed, experts, per):
    rows, cols = mixed.shape
    return call(
        functools.partial(dispatch_kernel, per),
        [jax.ShapeDtypeStruct((per, cols), bf16)] * experts,
        [SMEM, VMEM, VMEM],
        [VMEM] * experts,
        [],
        2 * rows * per * experts * cols,
        rows * cols * 2 + experts * per * cols * 2,
        where,
        slots,
        mixed,
    )


def up_kernel(pieces, weights, gain_ref, *refs):
    parts = refs[:pieces]
    ups = refs[pieces : pieces + weights]
    out = refs[pieces + weights]
    rows = parts[0].shape[0]
    tile = tile_of(rows)
    width = gain_ref.shape[1]

    def step(t, carry):
        at = pl.ds(pl.multiple_of(t * tile, tile), tile)
        values = jnp.concatenate([part[at].astype(f32) for part in parts], 1)
        center = values - jnp.sum(values, -1, keepdims=True) * (1.0 / width)
        spread = jnp.sum(center * center, -1, keepdims=True) * (1.0 / width)
        normed = (center * lax.rsqrt(spread + eps) * gain_ref[...]).astype(bf16)
        wide = ups[0].shape[1]
        for i, up in enumerate(ups):
            hidden = jnp.dot(normed, up[...], preferred_element_type=f32)
            out[at, i * wide : (i + 1) * wide] = jax.nn.gelu(hidden).astype(bf16)
        return carry

    lax.fori_loop(0, rows // tile, step, 0)


def up_project(parts, gain, ups):
    rows = parts[0].shape[0]
    wide = sum(up.shape[1] for up in ups)
    width = gain.shape[1]
    return call(
        functools.partial(up_kernel, len(parts), len(ups)),
        jax.ShapeDtypeStruct((rows, wide), bf16),
        [VMEM] * (1 + len(parts) + len(ups)),
        VMEM,
        [],
        2 * rows * width * wide,
        rows * (width + wide) * 2 + width * wide * 2,
        gain,
        *parts,
        *ups,
    )


def down_kernel(pieces, weights, blocks, *refs):
    hiddens = refs[:pieces]
    downs = refs[pieces : pieces + weights * blocks]
    outs = refs[pieces + weights * blocks :]
    base = 0
    for hidden in hiddens:
        rows = hidden.shape[0]
        tile = tile_of(rows)

        def step(t, carry, hidden=hidden, base=base, tile=tile):
            start = t * tile
            for d in range(blocks):
                deep = downs[d].shape[0]
                total = 0.0
                for i in range(weights):
                    total = total + jnp.dot(
                        hidden[
                            pl.ds(pl.multiple_of(start, tile), tile), i * deep : (i + 1) * deep
                        ],
                        downs[i * blocks + d][...],
                        preferred_element_type=f32,
                    )
                outs[d][pl.ds(pl.multiple_of(base + start, tile), tile)] = total.astype(bf16)
            return carry

        lax.fori_loop(0, rows // tile, step, 0)
        base += rows


def down_project(hiddens, downs):
    rows = sum(hidden.shape[0] for hidden in hiddens)
    blocks = len(downs[0])
    deep, cols = downs[0][0].shape
    flat = [block for group in downs for block in group]
    return call(
        functools.partial(down_kernel, len(hiddens), len(downs), blocks),
        [jax.ShapeDtypeStruct((rows, cols), bf16)] * blocks,
        [VMEM] * (len(hiddens) + len(flat)),
        [VMEM] * blocks,
        [],
        2 * rows * deep * len(downs) * cols * blocks,
        rows * deep * len(downs) * 2 + deep * len(downs) * cols * blocks * 2,
        *hiddens,
        *flat,
    )


def sum_kernel(pieces, parts, per, *refs):
    values, outs = refs[:pieces], refs[pieces:]
    experts = len(outs)
    for k, out in enumerate(outs):
        for h in range(parts):
            at = slice((h * experts + k) * per, (h * experts + k + 1) * per)
            total = values[0][at].astype(f32)
            for value in values[1:]:
                total = total + value[at].astype(f32)
            out[h * per : (h + 1) * per] = total.astype(bf16)


def sum_blocks(values, experts, parts, per):
    rows, cols = values[0].shape
    return call(
        functools.partial(sum_kernel, len(values), parts, per),
        [jax.ShapeDtypeStruct((parts * per, cols), bf16)] * experts,
        [VMEM] * len(values),
        [VMEM] * experts,
        [],
        rows * cols * 2,
        rows * cols * 2 * (len(values) + 1),
        *values,
    )


def combine_kernel(tables, first_col, where_ref, slot_ref, gate_ref, mixed_ref, *refs):
    sources, out, base, table, sems, base_sems = refs[:tables], *refs[tables:]
    cols = out.shape[1]
    blocks = where_ref.shape[0] - 3
    rows = out.shape[0] // blocks
    copies = []
    for i in range(blocks):
        start = pl.multiple_of(where_ref[3 + i] * rows, rows)
        copies.append(
            pltpu.make_async_copy(
                mixed_ref.at[pl.ds(start, rows), first_col : first_col + cols],
                base.at[i * rows : (i + 1) * rows],
                base_sems.at[i],
            )
        )
    many = sources[0].shape[0]
    for i, source in enumerate(sources):
        copies.append(
            pltpu.make_async_copy(source, table.at[i * many : (i + 1) * many], sems.at[i])
        )
    for copy in copies:
        copy.start()
    me, capacity, core = where_ref[0], where_ref[1], where_ref[2]
    half = capacity // tables
    slots = tables * many
    for copy in copies:
        copy.wait()
    tile = tile_of(out.shape[0])

    def step(t, carry):
        at = pl.ds(pl.multiple_of(t * tile, tile), tile)
        code = slot_ref[at]
        owner = code // capacity
        rank = code - owner * capacity
        part = rank // half
        place = jnp.where(
            code >= 0, (part ^ core) * many + (owner ^ me) * half + rank - part * half, -1
        )
        total = base[at].astype(f32)
        added = jnp.zeros((tile, cols), f32)
        lanes = lax.broadcasted_iota(jnp.int32, (tile, slots), 1)
        for k in range(code.shape[1]):
            hit = jnp.where(lanes == place[:, k : k + 1], 1.0, 0.0).astype(bf16)
            picked = jnp.dot(hit, table[...], preferred_element_type=f32)
            added = added + gate_ref[at, k : k + 1] * picked
        out[at] = (total + added).astype(bf16)
        return carry

    lax.fori_loop(0, out.shape[0] // tile, step, 0)


def combine(where, slots, gates, mixed, sources, first_col):
    blocks = where.shape[0] - 3
    rows = slots.shape[0]
    many, cols = sources[0].shape
    tables = len(sources)
    return call(
        functools.partial(combine_kernel, tables, first_col),
        jax.ShapeDtypeStruct((rows, cols), bf16),
        [SMEM, VMEM, VMEM, HBM] + [HBM] * tables,
        VMEM,
        [
            pltpu.VMEM((rows, cols), bf16),
            pltpu.VMEM((tables * many, cols), bf16),
            pltpu.SemaphoreType.DMA((tables,)),
            pltpu.SemaphoreType.DMA((blocks,)),
        ],
        4 * rows * many * tables * cols,
        rows * cols * 4 + tables * many * cols * 2,
        where,
        slots,
        gates,
        mixed,
        *sources,
    )


def qkv_kernel(groups, pieces, blocks, where_ref, gain_ref, weight_ref, *refs):
    streams, out = refs[: groups * pieces], refs[groups * pieces]
    rows = streams[0].shape[0] // blocks
    width = gain_ref.shape[1]
    tile = tile_of(rows)
    per = rows // tile
    heads = out.shape[2]

    for g in range(groups):

        def step(t, carry, g=g):
            block = t // per
            at = pl.ds(pl.multiple_of(t * tile, tile), tile)
            values = jnp.concatenate(
                [streams[g * pieces + i][at].astype(f32) for i in range(pieces)], 1
            )
            center = values - jnp.sum(values, -1, keepdims=True) * (1.0 / width)
            spread = jnp.sum(center * center, -1, keepdims=True) * (1.0 / width)
            normed = (center * lax.rsqrt(spread + eps) * gain_ref[...]).astype(bf16)
            result = jnp.dot(normed, weight_ref[...], preferred_element_type=f32).astype(bf16)
            start = where_ref[g * blocks + block] * rows + (t - block * per) * tile
            to = pl.ds(pl.multiple_of(start, tile), tile)
            for j in range(out.shape[0]):
                out[j, to] = result[:, j * heads : (j + 1) * heads]
            return carry

        lax.fori_loop(0, blocks * per, step, 0)


def qkv_project(where, gain, weight, streams, blocks):
    groups, pieces = len(streams), len(streams[0])
    flat = [piece for group in streams for piece in group]
    rows = sum(group[0].shape[0] for group in streams)
    width, wide = weight.shape
    return call(
        functools.partial(qkv_kernel, groups, pieces, blocks),
        jax.ShapeDtypeStruct((3, rows, wide // 3), bf16),
        [SMEM, VMEM, VMEM] + [VMEM] * len(flat),
        VMEM,
        [],
        2 * rows * width * wide,
        rows * (width + wide) * 2 + width * wide * 2,
        where,
        gain,
        weight,
        *flat,
    )


def local(
    tokens,
    time_taps,
    norm_gain,
    expert_ids,
    priority_ranks,
    keep_mask,
    gate_weights,
    up_weight,
    down_weight,
    attn_gain,
    qkv_weight,
):
    frames_here, patches, width = tokens.shape[1:]
    members = lax.axis_size("tm")
    experts = lax.axis_size("expert")
    chips = members // 2
    cols = width // chips
    place = lax.axis_index("tm")
    chip, core = place // 2, place % 2
    me = lax.axis_index("expert")
    own_rows = frames_here * patches
    rows = own_rows * members
    capacity = rows * expert_ids.shape[2] // (2 * experts)
    half = capacity // 2
    per = half // ROW_PARTS
    parts = column_parts(cols)

    def columns_of(value, d, at=0, size=cols):
        return lax.dynamic_slice_in_dim(value, (chip ^ d) * cols + at, size, value.ndim - 1)

    def by_share(value):
        return jnp.concatenate(
            [lax.dynamic_slice_in_dim(value, (chip ^ d) * cols, cols, 0) for d in range(chips)], 0
        )

    own_tokens = tokens.reshape(own_rows, width)
    mine = columns_of(own_tokens, 0)
    near = [mine] + [swap(columns_of(own_tokens, d), "tm", 2 * d) for d in range(1, chips)]
    over = [swap(value, "tm", 1) for value in near]
    near_places = [(chip ^ d) * 2 + core for d in range(chips)]
    over_places = [(chip ^ d) * 2 + 1 - core for d in range(chips)]

    up_mine = by_share(up_weight[0])
    ups = [up_mine, swap(up_mine, "tm", 1)]
    downs = []
    for at, size in parts:
        group = [columns_of(down_weight[0], d, at, size) for d in range(chips)]
        downs.append([group, [swap(block, "tm", 1) for block in group]])
    gain_up = by_share(norm_gain)[None]
    gain_qkv = by_share(attn_gain)[None]
    qkv_mine = by_share(jnp.swapaxes(qkv_weight, 0, 1).reshape(width, -1))
    taps = columns_of(time_taps, 0)

    code = jnp.where(keep_mask[0] == 1, expert_ids[0] * capacity + priority_ranks[0], -1)
    token_places = jnp.stack(near_places + over_places).astype(jnp.int32)
    mixed = temporal_mix(near + over, token_places, taps, patches)

    code_rows = code.T
    hiddens = []
    for h in range(ROW_PARTS):
        where = jnp.stack([me, jnp.int32(capacity), core * half + h * per]).astype(jnp.int32)
        blocks = dispatch(where, code_rows, mixed, experts, per)
        arrived = jnp.concatenate(
            [blocks[0]] + [swap(blocks[k], "expert", k) for k in range(1, experts)], 0
        )
        shares = [arrived] + [swap(arrived, "tm", 2 * d) for d in range(1, chips)]
        hiddens.append(up_project(shares, gain_up, ups))

    block_places = jnp.stack([i * 2 + core for i in range(chips)]).astype(jnp.int32)
    where = jnp.concatenate(
        [jnp.stack([me, jnp.int32(capacity), core]).astype(jnp.int32), block_places]
    )

    def rows_of(value):
        shaped = value.reshape(chips, 2, own_rows, -1)
        return lax.dynamic_index_in_dim(shaped, core, 1, keepdims=False).reshape(
            chips * own_rows, -1
        )

    code_here = rows_of(code)
    gates_here = rows_of(gate_weights[0])
    here = [[None] * len(parts) for _ in range(chips)]
    there = [[None] * len(parts) for _ in range(chips)]
    for q, (at, size) in enumerate(parts):
        sums = down_project(hiddens, downs[q])
        pieces = [sums[0]] + [swap(sums[d], "tm", 2 * d) for d in range(1, chips)]
        outgoing = sum_blocks(pieces, experts, ROW_PARTS, per)
        returned = jnp.concatenate(
            [outgoing[0]] + [swap(outgoing[k], "expert", k) for k in range(1, experts)], 0
        )
        tables = [returned, swap(returned, "tm", 1)]
        stream = combine(where, code_here, gates_here, mixed, tables, at)
        for d in range(chips):
            here[d][q] = stream if d == 0 else swap(stream, "tm", 2 * d)
            there[d][q] = swap(here[d][q], "tm", 1)

    streams = [sum(here, []), sum(there, [])]
    order = jnp.stack(
        [i * 2 + core for i in range(chips)] + [i * 2 + 1 - core for i in range(chips)]
    ).astype(jnp.int32)
    qkv_rows = qkv_project(order, gain_qkv, qkv_mine, streams, chips)[:, None]

    own = [
        jnp.concatenate(
            [lax.dynamic_slice_in_dim(v, chip * own_rows, own_rows, 0) for v in here[d]], 1
        )
        for d in range(chips)
    ]
    stacked = jnp.stack(own)
    stream_here = jnp.concatenate([stacked[chip ^ i] for i in range(chips)], 1)
    return (stream_here.reshape(tokens.shape), qkv_rows)


def solution(mesh):
    in_specs = (
        P("expert", "tm", None, None),
        P(),
        P(),
        P("expert", None, None),
        P("expert", None, None),
        P("expert", None, None),
        P("expert", None, None),
        P("expert", None, "tm"),
        P("expert", "tm", None),
        P(),
        P(None, None, "tm"),
    )
    out_specs = (P("expert", "tm", None, None), P(None, "expert", None, "tm"))
    return jax.shard_map(local, mesh=mesh, in_specs=in_specs, out_specs=out_specs, check_vma=False)
```

time: 553 us -> 281 us (0.51)
  blocking collectives: 159 us -> 0 us
  other arithmetic: 143 us -> 6.46 us
  Pallas kernels: 0 us -> 109 us
  waiting for transfers between devices: 114 us -> 49.6 us
  starting transfers between devices: 2.5 us -> 61.6 us
  local copies, waits for them, and re-layouts: 98.1 us -> 52 us
  matrix products: 22.7 us -> 0 us
  between operations: 14 us -> 1.09 us
    all_to_all x2 -> x0, blocking collectives: 159 us -> none  [the longest x1 122 us: local(): lax.all_to_all(outgoing, 'expert', split_axis=0, concat_axis=0, tiled=True)]
    reduce_sum x5 -> x0, other arithmetic: 132 us -> none  [the longest x1 111 us: local(): jnp.sum(weight[:, :, None] * picked.astype(jnp.float32), 1)]
    pallas_call x0 -> x12, Pallas kernels: none -> 109 us  [call(): pl.pallas_call(kernel, out_shape=out_shape, in_specs=in_specs, out_specs=...]
    all_gather x2 -> x0, waiting for transfers between devices: 63.8 us -> none  [the longest x1 37.4 us: local(): expert_out = lax.all_gather(returned, 'tm', axis=1, tiled=True)]
    ppermute x1 -> x48, starting transfers between devices: 2.38 us -> 61.6 us  [swap(): return lax.ppermute(value, axis, [(i, i ^ distance) for i in range(count)])]
    reduce_scatter x1 -> x0, waiting for transfers between devices: 49.6 us -> none  [local(): lax.psum_scatter(partial_value.astype(jnp.bfloat16), 'tm', scatter_dimens...]
    ppermute x1 -> x48, waiting for transfers between devices: 0.33 us -> 49.6 us  [swap(): return lax.ppermute(value, axis, [(i, i ^ distance) for i in range(count)])]
    gather x2 -> x0, local copies, waits for them, and re-layouts: 41.4 us -> none  [the longest x1 26.1 us: local(): picked = table[slot_index]]
  transfers between devices with their start and end apart: 4 -> 48, of which waited for: 4 -> 18; matrix products, arithmetic and copies ran while one was open for 4% -> 15% of each run, Pallas kernels for 0% -> 33%
where the time goes in v1:
time: 281 us; the launch traced here: 280 us
  Pallas kernels  109 us (39%)
  starting transfers between devices  61.6 us (22%)
  local copies, waits for them, and re-layouts  52 us (19%)
  waiting for transfers between devices  49.6 us (18%)
  other arithmetic  6.46 us (2%)
    pallas_call x12, Pallas kernels, call(): pl.pallas_call(kernel, out_shape=out_shape, in_specs=in_specs, out_specs=...  109 us
    ppermute x48, starting transfers between devices, swap(): return lax.ppermute(value, axis, [(i, i ^ distance) for i in range(count)])  61.6 us
    ppermute x48, waiting for transfers between devices, swap(): return lax.ppermute(value, axis, [(i, i ^ distance) for i in range(count)])  49.6 us
    unnamed x97, local copies, waits for them, and re-layouts  35.7 us
    dynamic_slice x4, local copies, waits for them, and re-layouts, columns_of(): lax.dynamic_slice_in_dim(value, (chip ^ d) * cols + at, size, value.ndim...  7.29 us
  transfers between devices with their start and end apart: 48, of which 18 were waited for; matrix products, arithmetic and copies ran while one was open for 15% of the time, Pallas kernels for 33%

profile of v1, /device:TPU:0, one launch (start us, length us, event | category | flops | bytes accessed | tf_op | source)
XLA Modules:
  0.0 279.8 jit_solution(10756888362505422274)
XLA Ops:
  3.1 2.9 %collective-permute-start = (bf16[512,640]{1,0:T(8,128)(2,1)}, bf16[512,640]{1,0:T(8,128)(2,1)}, u32[]{:S(2)}, u32[]{:S(2)}) collective-permute-start(bf16[512,640]{1,0:T(8,128)(2,1)} %get-tuple-element.88), channel_id=1, source_target_pairs={{0,16},{8,24},{16,0},{24,8},{1,17},{9,25},{17,1},{25,9},{2,18},{10... | collective-permute-start | bytes 1966088 | tf_op jit(solution)/shard_map/ppermute | solution.py:39
  9.1 3.0 %dynamic-slice_bitcast_fusion.4 = (bf16[1280,256]{1,0:T(8,128)(2,1)}, bf16[1280,256]{1,0:T(8,128)(2,1)}) fusion(bf16[1,1280,1280]{2,1,0:T(8,128)(2,1)} %param.19, s32[]{:T(128)S(6)} %select_n.73, s32[]{:T(128)S(6)} %select_n.72), kind=kLoop, calls=%fused_computation.15 | loop fusion | bytes 2621448 | tf_op jit(solution)/shard_map/dynamic_slice | solution.py:401
  13.9 7.3 %collective-permute-done.refs_1_ = bf16[512,640]{1,0:T(8,128)(2,1)} collective-permute-done((bf16[512,640]{1,0:T(8,128)(2,1)}, bf16[512,640]{1,0:T(8,128)(2,1)}, u32[]{:S(2)}, u32[]{:S(2)}) %collective-permute-start) | collective-permute-done | bytes 655392 | tf_op jit(solution)/shard_map/ppermute | solution.py:39
  24.3 5.7 %shard_map.122.mixed_ref = bf16[2048,640]{1,0:T(8,128)(2,1)} custom-call(s32[4]{0:T(128)} %pad_add_fusion.where_ref, f32[3,640]{1,0:T(4,128)} %constant_dynamic-slice_fusion.8.taps_ref, bf16[512,640]{1,0:T(8,128)(2,1)} %get-tuple-element.89.refs_0_, bf16[512,640]{1,0:T(8,128)(2,1)} %collective-permute-done.refs_1_, ...), custom_call_target="tpu_custom_call" | custom-call | flops 6553600 | bytes 5242880 | tf_op jit(solution)/shard_map/pallas_call | solution.py:26
  29.9 4.4 %shard_map.125 = (bf16[64,640]{1,0:T(8,128)(2,1)}, bf16[64,640]{1,0:T(8,128)(2,1)}, bf16[64,640]{1,0:T(8,128)(2,1)}, bf16[64,640]{1,0:T(8,128)(2,1)}, bf16[64,64...) custom-call(s32[3]{0:T(128)} %get-tuple-element.95.where_ref, ...), custom_call_target="tpu_custom_call" | custom-call | flops 1342177280 | bytes 3276800 | tf_op jit(solution)/shard_map/pallas_call | solution.py:26
  39.3 4.6 %shard_map.123 = (bf16[64,640]{1,0:T(8,128)(2,1)}, bf16[64,640]{1,0:T(8,128)(2,1)}, bf16[64,640]{1,0:T(8,128)(2,1)}, bf16[64,640]{1,0:T(8,128)(2,1)}, bf16[64,64...) custom-call(s32[3]{0:T(128)} %get-tuple-element.94.where_ref, ...), custom_call_target="tpu_custom_call" | custom-call | flops 1342177280 | bytes 3276800 | tf_op jit(solution)/shard_map/pallas_call | solution.py:26
  46.1 2.8 %collective-permute-start.15 = (bf16[64,640]{1,0:T(8,128)(2,1)S(1)}, bf16[64,640]{1,0:T(8,128)(2,1)S(1)}, u32[]{:S(2)}, u32[]{:S(2)}) collective-permute-start(bf16[64,640]{1,0:T(8,128)(2,1)S(1)} %copy-done.30), channel_id=1, source_target_pairs={{0,4},{1,5},{2,6},{3,7},{4,0},{5,1},{6,2},{7,3},{8,12},{9,13},{10,... | collective-permute-start | bytes 245768 | tf_op jit(solution)/shard_map/ppermute | solution.py:39
  54.2 3.7 %collective-permute-start.17 = (bf16[64,640]{1,0:T(8,128)(2,1)S(1)}, bf16[64,640]{1,0:T(8,128)(2,1)S(1)}, u32[]{:S(2)}, u32[]{:S(2)}) collective-permute-start(bf16[64,640]{1,0:T(8,128)(2,1)S(1)} %copy-done.28), channel_id=1, source_target_pairs={{0,6},{1,7},{2,4},{3,5},{4,2},{5,3},{6,0},{7,1},{8,14},{9,15},{10,... | collective-permute-start | bytes 245768 | tf_op jit(solution)/shard_map/ppermute | solution.py:39
  74.8 2.7 collective-permute-start.7
  89.1 4.2 %collective-permute-done.9 = bf16[64,640]{1,0:T(8,128)(2,1)S(1)} collective-permute-done((bf16[64,640]{1,0:T(8,128)(2,1)}, bf16[64,640]{1,0:T(8,128)(2,1)S(1)}, u32[]{:S(2)}, u32[]{:S(2)}) %collective-permute-start.9) | collective-permute-done | bytes 81952 | tf_op jit(solution)/shard_map/ppermute | solution.py:39
  99.2 9.9 %shard_map.126.refs_1_ = bf16[512,2560]{1,0:T(8,128)(2,1)} custom-call(f32[1,1280]{1,0:T(1,128)} %broadcast_in_dim.14.gain_ref, bf16[512,640]{1,0:T(8,128)(2,1)} %constant_dynamic-update-slice_fusion.8.refs_0_, bf16[512,640]{1,0:T(8,128)(2,1)} %copy-done.24, bf16[1280,1280]{1,0:T(8,128)(2,1)} %copy-done.2, bf16[1280,1280]{1,0:T(8,128)(2,1)} %collective-permute-done.11.refs_3_), custom_call_target="tpu_custom_call" | custom-call | flops 3355443200 | bytes 10485760 | tf_op jit(solution)/shard_map/pallas_call | solution.py:26
  109.1 9.8 %shard_map.124.refs_0_ = bf16[512,2560]{1,0:T(8,128)(2,1)} custom-call(f32[1,1280]{1,0:T(1,128)} %broadcast_in_dim.14.gain_ref, bf16[512,640]{1,0:T(8,128)(2,1)} %constant_dynamic-update-slice_fusion.refs_0_, bf16[512,640]{1,0:T(8,128)(2,1)} %collective-permute-done.10.refs_1_, bf16[1280,1280]{1,0:T(8,128)(2,1)} %copy-done.2, ...), custom_call_target="tpu_custom_call" | custom-call | flops 3355443200 | bytes 10485760 | tf_op jit(solution)/shard_map/pallas_call | solution.py:26
  118.9 7.6 %shard_map.130 = (bf16[1024,256]{1,0:T(8,128)(2,1)}, bf16[1024,256]{1,0:T(8,128)(2,1)}) custom-call(bf16[512,2560]{1,0:T(8,128)(2,1)} %shard_map.124.refs_0_, bf16[512,2560]{1,0:T(8,128)(2,1)} %shard_map.126.refs_1_, bf16[1280,256]{1,0:T(8,128)(2,1)} %get-tuple-element.81.refs_2_, bf16[1280,256]{1,0:T(8,128)(2,1)} %get-tuple-element.80.refs_3_, ...), custom_call_target="tpu_custom_call" | custom-call | flops 2684354560 | bytes 7864320 | tf_op jit(solution)/shard_map/pallas_call | solution.py:26
  130.6 10.7 %shard_map.127 = (bf16[1024,384]{1,0:T(8,128)(2,1)}, bf16[1024,384]{1,0:T(8,128)(2,1)}) custom-call(bf16[512,2560]{1,0:T(8,128)(2,1)} %shard_map.124.refs_0_, bf16[512,2560]{1,0:T(8,128)(2,1)} %shard_map.126.refs_1_, bf16[1280,384]{1,0:T(8,128)(2,1)} %get-tuple-element.79.refs_2_, bf16[1280,384]{1,0:T(8,128)(2,1)} %copy-done.4, ...), custom_call_target="tpu_custom_call" | custom-call | flops 4026531840 | bytes 9175040 | tf_op jit(solution)/shard_map/pallas_call | solution.py:26
  151.4 4.4 %collective-permute-start.39 = (bf16[128,256]{1,0:T(8,128)(2,1)}, bf16[128,256]{1,0:T(8,128)(2,1)S(1)}, u32[]{:S(2)}, u32[]{:S(2)}) collective-permute-start(bf16[128,256]{1,0:T(8,128)(2,1)} %get-tuple-element.72), channel_id=1, source_target_pairs={{0,6},{1,7},{2,4},{3,5},{4,2},{5,3},{6,0},{7,1},{8,14},{9,15},{10,... | collective-permute-start | bytes 196616 | tf_op jit(solution)/shard_map/ppermute | solution.py:39
  156.5 3.1 %collective-permute-done.38 = bf16[128,256]{1,0:T(8,128)(2,1)S(1)} collective-permute-done((bf16[128,256]{1,0:T(8,128)(2,1)}, bf16[128,256]{1,0:T(8,128)(2,1)S(1)}, u32[]{:S(2)}, u32[]{:S(2)}) %collective-permute-start.38) | collective-permute-done | bytes 65568 | tf_op jit(solution)/shard_map/ppermute | solution.py:39
  173.2 3.3 %collective-permute-start.28 = (bf16[128,384]{1,0:T(8,128)(2,1)}, bf16[128,384]{1,0:T(8,128)(2,1)S(1)}, u32[]{:S(2)}, u32[]{:S(2)}) collective-permute-start(bf16[128,384]{1,0:T(8,128)(2,1)} %get-tuple-element.62), channel_id=1, source_target_pairs={{0,6},{1,7},{2,4},{3,5},{4,2},{5,3},{6,0},{7,1},{8,14},{9,15},{10,... | collective-permute-start | bytes 294920 | tf_op jit(solution)/shard_map/ppermute | solution.py:39
  179.6 5.3 %collective-permute-done.27 = bf16[128,384]{1,0:T(8,128)(2,1)S(1)} collective-permute-done((bf16[128,384]{1,0:T(8,128)(2,1)}, bf16[128,384]{1,0:T(8,128)(2,1)S(1)}, u32[]{:S(2)}, u32[]{:S(2)}) %collective-permute-start.27) | collective-permute-done | bytes 98336 | tf_op jit(solution)/shard_map/ppermute | solution.py:39
  189.7 2.9 %constant_dynamic-slice_fusion.1 = (bf16[640,960]{0,1:T(8,128)(2,1)S(1)}, bf16[640,960]{0,1:T(8,128)(2,1)}) fusion(bf16[1280,960]{0,1:T(8,128)(2,1)} %bitcast.46, s32[]{:T(128)S(6)} %select_n.68, s32[]{:T(128)S(6)} %select_n.69), kind=kLoop, calls=%fused_computation.53 | loop fusion | bytes 4915208 | tf_op jit(solution)/shard_map/dynamic_slice | solution.py:405
  196.5 17.0 %shard_map.132.refs_1_ = bf16[1024,256]{1,0:T(8,128)(2,1)} custom-call(s32[5]{0:T(128)} %concatenate.41.where_ref, s32[1024,2]{1,0:T(8,128)} %bitcast.50, f32[1024,2]{1,0:T(8,128)} %bitcast.48, bf16[2048,640]{1,0:T(8,128)(2,1)} %shard_map.122.mixed_ref, bf16[1024,256]{1,0:T(8,128)(2,1)} %copy-done.17, bf16[1024,256]{1,0:T(8,128)(2,1)} %collective-permute-done.41.refs_1_), custom_call_target="tpu_custom_call" | custom-call | flops 2147483648 | bytes 2097152 | tf_op jit(solution)/shard_map/pallas_call | solution.py:26
  214.5 19.7 %shard_map.129.refs_0_ = bf16[1024,384]{1,0:T(8,128)(2,1)} custom-call(s32[5]{0:T(128)} %concatenate.41.where_ref, s32[1024,2]{1,0:T(8,128)} %bitcast.51, f32[1024,2]{1,0:T(8,128)} %bitcast.49, bf16[2048,640]{1,0:T(8,128)(2,1)} %shard_map.122.mixed_ref, bf16[1024,384]{1,0:T(8,128)(2,1)} %constant_dynamic-update-slice_fusion.16.refs_0_, ...), custom_call_target="tpu_custom_call" | custom-call | flops 3221225472 | bytes 3145728 | tf_op jit(solution)/shard_map/pallas_call | solution.py:26
  238.7 15.0 %collective-permute-done.42.refs_2_ = bf16[1024,384]{1,0:T(8,128)(2,1)S(1)} collective-permute-done((bf16[1024,384]{1,0:T(8,128)(2,1)}, bf16[1024,384]{1,0:T(8,128)(2,1)S(1)}, u32[]{:S(2)}, u32[]{:S(2)}) %collective-permute-start.42) | collective-permute-done | bytes 786464 | tf_op jit(solution)/shard_map/ppermute | solution.py:39
  257.9 15.5 %shard_map.133 = bf16[3,2048,320]{2,1,0:T(8,128)(2,1)} custom-call(s32[4]{0:T(128)} %pad_add_fusion.4.where_ref, f32[1,1280]{1,0:T(1,128)} %broadcast_in_dim.15.gain_ref, bf16[1280,960]{1,0:T(8,128)(2,1)} %pad_maximum_fusion.1.weight_ref, bf16[1024,384]{1,0:T(8,128)(2,1)} %shard_map.129.refs_0_, bf16[1024,256]{1,0:T(8,128)(2,1)} %shard_map.132.refs_1_, ...), custom_call_target="tpu_custom_call" | custom-call | flops 5033164800 | bytes 11632640 | tf_op jit(solution)/shard_map/pallas_call | solution.py:26
  273.4 6.4 %copy.21 = bf16[3,1,2048,320]{2,3,1,0:T(8,128)(2,1)} copy(bf16[3,1,2048,320]{3,2,0,1:T(8,128)(2,1)} %bitcast.43) | data formatting | bytes 7864320
  (215 shorter events, 107.0 us)
Async XLA Ops:
  3.1 18.0 %collective-permute-start = (bf16[512,640]{1,0:T(8,128)(2,1)}, bf16[512,640]{1,0:T(8,128)(2,1)}, u32[]{:S(2)}, u32[]{:S(2)}) collective-permute-start(bf16[512,640]{1,0:T(8,128)(2,1)} %get-tuple-element.88), channel_id=1, source_target_pairs={{0,16},{8,24},{16,0},{24,8},{1,17},{9,25},{17,1},{25,9},{2,18},{10... | collective-permute-start | bytes 1966088 | tf_op jit(solution)/shard_map/ppermute | solution.py:39
  6.1 16.4 %collective-permute-start.1 = (bf16[512,640]{1,0:T(8,128)(2,1)}, bf16[512,640]{1,0:T(8,128)(2,1)}, u32[]{:S(2)}, u32[]{:S(2)}) collective-permute-start(bf16[512,640]{1,0:T(8,128)(2,1)} %get-tuple-element.89.refs_0_), channel_id=1, source_target_pairs={{0,8},{8,0},{16,24},{24,16},{1,9},{9,1},{17,25},{25,17},{2,10},{10... | collective-permute-start | bytes 1966088 | tf_op jit(solution)/shard_map/ppermute | solution.py:39
  8.5 89.9 %collective-permute-start.11 = (bf16[1280,1280]{1,0:T(8,128)(2,1)S(1)}, bf16[1280,1280]{1,0:T(8,128)(2,1)}, u32[]{:S(2)}, u32[]{:S(2)}) collective-permute-start(bf16[1280,1280]{1,0:T(8,128)(2,1)S(1)} %pad_maximum_fusion.refs_2_), channel_id=1, source_target_pairs={{0,8},{8,0},{16,24},{24,16},{1,9},{9,1},{17,25},{25,17},{2,10},{10... | collective-permute-start | bytes 9830408 | tf_op jit(solution)/shard_map/ppermute | solution.py:39
  12.1 106.8 %collective-permute-start.31 = (bf16[1280,256]{1,0:T(8,128)(2,1)}, bf16[1280,256]{1,0:T(8,128)(2,1)}, u32[]{:S(2)}, u32[]{:S(2)}) collective-permute-start(bf16[1280,256]{1,0:T(8,128)(2,1)} %get-tuple-element.81.refs_2_), channel_id=1, source_target_pairs={{0,8},{8,0},{16,24},{24,16},{1,9},{9,1},{17,25},{25,17},{2,10},{10... | collective-permute-start | bytes 1966088 | tf_op jit(solution)/shard_map/ppermute | solution.py:39
  12.6 106.3 %collective-permute-start.32 = (bf16[1280,256]{1,0:T(8,128)(2,1)}, bf16[1280,256]{1,0:T(8,128)(2,1)}, u32[]{:S(2)}, u32[]{:S(2)}) collective-permute-start(bf16[1280,256]{1,0:T(8,128)(2,1)} %get-tuple-element.80.refs_3_), channel_id=1, source_target_pairs={{0,8},{8,0},{16,24},{24,16},{1,9},{9,1},{17,25},{25,17},{2,10},{10... | collective-permute-start | bytes 1966088 | tf_op jit(solution)/shard_map/ppermute | solution.py:39
  34.3 11.0 %collective-permute-start.12 = (bf16[64,640]{1,0:T(8,128)(2,1)}, bf16[64,640]{1,0:T(8,128)(2,1)S(1)}, u32[]{:S(2)}, u32[]{:S(2)}) collective-permute-start(bf16[64,640]{1,0:T(8,128)(2,1)} %get-tuple-element.47), channel_id=1, source_target_pairs={{0,1},{1,0},{2,3},{3,2},{4,5},{5,4},{6,7},{7,6},{8,9},{9,8},{10,11... | collective-permute-start | bytes 245768 | tf_op jit(solution)/shard_map/ppermute | solution.py:39
  36.1 10.0 %collective-permute-start.13 = (bf16[64,640]{1,0:T(8,128)(2,1)}, bf16[64,640]{1,0:T(8,128)(2,1)S(1)}, u32[]{:S(2)}, u32[]{:S(2)}) collective-permute-start(bf16[64,640]{1,0:T(8,128)(2,1)} %get-tuple-element.48), channel_id=1, source_target_pairs={{0,2},{1,3},{2,0},{3,1},{4,6},{5,7},{6,4},{7,5},{8,10},{9,11},{10,... | collective-permute-start | bytes 245768 | tf_op jit(solution)/shard_map/ppermute | solution.py:39
  82.3 16.1 %collective-permute-start.19 = (bf16[512,640]{1,0:T(8,128)(2,1)}, bf16[512,640]{1,0:T(8,128)(2,1)S(1)}, u32[]{:S(2)}, u32[]{:S(2)}) collective-permute-start(bf16[512,640]{1,0:T(8,128)(2,1)} %constant_dynamic-update-slice_fusion.8.refs_0_), channel_id=1, source_target_pairs={{0,16},{8,24},{16,0},{24,8},{1,17},{9,25},{17,1},{25,9},{2,18},{10... | collective-permute-start | bytes 1966088 | tf_op jit(solution)/shard_map/ppermute | solution.py:39
  93.9 15.3 %collective-permute-start.10 = (bf16[512,640]{1,0:T(8,128)(2,1)}, bf16[512,640]{1,0:T(8,128)(2,1)}, u32[]{:S(2)}, u32[]{:S(2)}) collective-permute-start(bf16[512,640]{1,0:T(8,128)(2,1)} %constant_dynamic-update-slice_fusion.refs_0_), channel_id=1, source_target_pairs={{0,16},{8,24},{16,0},{24,8},{1,17},{9,25},{17,1},{25,9},{2,18},{10... | collective-permute-start | bytes 1966088 | tf_op jit(solution)/shard_map/ppermute | solution.py:39
  98.4 30.3 %collective-permute-start.20 = (bf16[1280,384]{1,0:T(8,128)(2,1)}, bf16[1280,384]{1,0:T(8,128)(2,1)S(1)}, u32[]{:S(2)}, u32[]{:S(2)}) collective-permute-start(bf16[1280,384]{1,0:T(8,128)(2,1)} %get-tuple-element.79.refs_2_), channel_id=1, source_target_pairs={{0,8},{8,0},{16,24},{24,16},{1,9},{9,1},{17,25},{25,17},{2,10},{10... | collective-permute-start | bytes 2949128 | tf_op jit(solution)/shard_map/ppermute | solution.py:39
  99.2 29.4 %collective-permute-start.21 = (bf16[1280,384]{1,0:T(8,128)(2,1)S(1)}, bf16[1280,384]{1,0:T(8,128)(2,1)S(1)}, u32[]{:S(2)}, u32[]{:S(2)}) collective-permute-start(bf16[1280,384]{1,0:T(8,128)(2,1)S(1)} %get-tuple-element.78.refs_3_), channel_id=1, source_target_pairs={{0,8},{8,0},{16,24},{24,16},{1,9},{9,1},{17,25},{25,17},{2,10},{10... | collective-permute-start | bytes 2949128 | tf_op jit(solution)/shard_map/ppermute | solution.py:39
  126.5 15.0 %collective-permute-start.33 = (bf16[1024,256]{1,0:T(8,128)(2,1)}, bf16[1024,256]{1,0:T(8,128)(2,1)S(1)}, u32[]{:S(2)}, u32[]{:S(2)}) collective-permute-start(bf16[1024,256]{1,0:T(8,128)(2,1)} %get-tuple-element.65), channel_id=1, source_target_pairs={{0,16},{8,24},{16,0},{24,8},{1,17},{9,25},{17,1},{25,9},{2,18},{10... | collective-permute-start | bytes 1572872 | tf_op jit(solution)/shard_map/ppermute | solution.py:39
  141.2 19.9 %collective-permute-start.22 = (bf16[1024,384]{1,0:T(8,128)(2,1)}, bf16[1024,384]{1,0:T(8,128)(2,1)S(1)}, u32[]{:S(2)}, u32[]{:S(2)}) collective-permute-start(bf16[1024,384]{1,0:T(8,128)(2,1)} %get-tuple-element.55), channel_id=1, source_target_pairs={{0,16},{8,24},{16,0},{24,8},{1,17},{9,25},{17,1},{25,9},{2,18},{10... | collective-permute-start | bytes 2359304 | tf_op jit(solution)/shard_map/ppermute | solution.py:39
  155.8 30.9 %collective-permute-start.40 = (bf16[128,256]{1,0:T(8,128)(2,1)}, bf16[128,256]{1,0:T(8,128)(2,1)S(1)}, u32[]{:S(2)}, u32[]{:S(2)}) collective-permute-start(bf16[128,256]{1,0:T(8,128)(2,1)} %get-tuple-element.73), channel_id=1, source_target_pairs={{0,7},{1,6},{2,5},{3,4},{4,3},{5,2},{6,1},{7,0},{8,15},{9,14},{10,... | collective-permute-start | bytes 196616 | tf_op jit(solution)/shard_map/ppermute | solution.py:39
  166.1 11.0 %collective-permute-start.25 = (bf16[128,384]{1,0:T(8,128)(2,1)}, bf16[128,384]{1,0:T(8,128)(2,1)S(1)}, u32[]{:S(2)}, u32[]{:S(2)}) collective-permute-start(bf16[128,384]{1,0:T(8,128)(2,1)} %get-tuple-element.59), channel_id=1, source_target_pairs={{0,3},{1,2},{2,1},{3,0},{4,7},{5,6},{6,5},{7,4},{8,11},{9,10},{10,... | collective-permute-start | bytes 294920 | tf_op jit(solution)/shard_map/ppermute | solution.py:39
  167.8 11.2 %collective-permute-start.26 = (bf16[128,384]{1,0:T(8,128)(2,1)}, bf16[128,384]{1,0:T(8,128)(2,1)S(1)}, u32[]{:S(2)}, u32[]{:S(2)}) collective-permute-start(bf16[128,384]{1,0:T(8,128)(2,1)} %get-tuple-element.60), channel_id=1, source_target_pairs={{0,4},{1,5},{2,6},{3,7},{4,0},{5,1},{6,2},{7,3},{8,12},{9,13},{10,... | collective-permute-start | bytes 294920 | tf_op jit(solution)/shard_map/ppermute | solution.py:39
  171.8 13.0 %collective-permute-start.27 = (bf16[128,384]{1,0:T(8,128)(2,1)}, bf16[128,384]{1,0:T(8,128)(2,1)S(1)}, u32[]{:S(2)}, u32[]{:S(2)}) collective-permute-start(bf16[128,384]{1,0:T(8,128)(2,1)} %get-tuple-element.61), channel_id=1, source_target_pairs={{0,5},{1,4},{2,7},{3,6},{4,1},{5,0},{6,3},{7,2},{8,13},{9,12},{10,... | collective-permute-start | bytes 294920 | tf_op jit(solution)/shard_map/ppermute | solution.py:39
  173.2 12.3 %collective-permute-start.28 = (bf16[128,384]{1,0:T(8,128)(2,1)}, bf16[128,384]{1,0:T(8,128)(2,1)S(1)}, u32[]{:S(2)}, u32[]{:S(2)}) collective-permute-start(bf16[128,384]{1,0:T(8,128)(2,1)} %get-tuple-element.62), channel_id=1, source_target_pairs={{0,6},{1,7},{2,4},{3,5},{4,2},{5,3},{6,0},{7,1},{8,14},{9,15},{10,... | collective-permute-start | bytes 294920 | tf_op jit(solution)/shard_map/ppermute | solution.py:39
  186.8 27.7 %collective-permute-start.30 = (bf16[1024,384]{1,0:T(8,128)(2,1)}, bf16[1024,384]{1,0:T(8,128)(2,1)}, u32[]{:S(2)}, u32[]{:S(2)}) collective-permute-start(bf16[1024,384]{1,0:T(8,128)(2,1)} %constant_dynamic-update-slice_fusion.16.refs_0_), channel_id=1, source_target_pairs={{0,8},{8,0},{16,24},{24,16},{1,9},{9,1},{17,25},{25,17},{2,10},{10... | collective-permute-start | bytes 2359304 | tf_op jit(solution)/shard_map/ppermute | solution.py:39
  213.5 24.4 %collective-permute-start.43 = (bf16[1024,256]{1,0:T(8,128)(2,1)}, bf16[1024,256]{1,0:T(8,128)(2,1)S(1)}, u32[]{:S(2)}, u32[]{:S(2)}) collective-permute-start(bf16[1024,256]{1,0:T(8,128)(2,1)} %shard_map.132.refs_1_), channel_id=1, source_target_pairs={{0,16},{8,24},{16,0},{24,8},{1,17},{9,25},{17,1},{25,9},{2,18},{10... | collective-permute-start | bytes 1572872 | tf_op jit(solution)/shard_map/ppermute | solution.py:39
  234.2 19.5 %collective-permute-start.42 = (bf16[1024,384]{1,0:T(8,128)(2,1)}, bf16[1024,384]{1,0:T(8,128)(2,1)S(1)}, u32[]{:S(2)}, u32[]{:S(2)}) collective-permute-start(bf16[1024,384]{1,0:T(8,128)(2,1)} %shard_map.129.refs_0_), channel_id=1, source_target_pairs={{0,16},{8,24},{16,0},{24,8},{1,17},{9,25},{17,1},{25,9},{2,18},{10... | collective-permute-start | bytes 2359304 | tf_op jit(solution)/shard_map/ppermute | solution.py:39
  237.9 17.8 %collective-permute-start.45 = (bf16[1024,256]{1,0:T(8,128)(2,1)S(1)}, bf16[1024,256]{1,0:T(8,128)(2,1)S(1)}, u32[]{:S(2)}, u32[]{:S(2)}) collective-permute-start(bf16[1024,256]{1,0:T(8,128)(2,1)S(1)} %copy-done.10), channel_id=1, source_target_pairs={{0,8},{8,0},{16,24},{24,16},{1,9},{9,1},{17,25},{25,17},{2,10},{10... | collective-permute-start | bytes 1572872 | tf_op jit(solution)/shard_map/ppermute | solution.py:39
  237.9 17.8 %collective-permute-start.47 = (bf16[1024,256]{1,0:T(8,128)(2,1)S(1)}, bf16[1024,256]{1,0:T(8,128)(2,1)S(1)}, u32[]{:S(2)}, u32[]{:S(2)}) collective-permute-start(bf16[1024,256]{1,0:T(8,128)(2,1)S(1)} %collective-permute-done.43.refs_3_), channel_id=1, source_target_pairs={{0,8},{8,0},{16,24},{24,16},{1,9},{9,1},{17,25},{25,17},{2,10},{10... | collective-permute-start | bytes 1572872 | tf_op jit(solution)/shard_map/ppermute | solution.py:39
  238.5 17.2 %collective-permute-start.44 = (bf16[1024,384]{1,0:T(8,128)(2,1)S(1)}, bf16[1024,384]{1,0:T(8,128)(2,1)S(1)}, u32[]{:S(2)}, u32[]{:S(2)}) collective-permute-start(bf16[1024,384]{1,0:T(8,128)(2,1)S(1)} %copy-done.8), channel_id=1, source_target_pairs={{0,8},{8,0},{16,24},{24,16},{1,9},{9,1},{17,25},{25,17},{2,10},{10... | collective-permute-start | bytes 2359304 | tf_op jit(solution)/shard_map/ppermute | solution.py:39
  (56 other events, 534.7 us)
